TPU v7x, 32 devices: a whole 2x2x4 slice. The times are simulated.
32 devices in a mesh: node: 1, group: 32 (over z, y, x, core), fsdp: 1.
Axes of the slice: x: 2, y: 2, z: 4, core: 2. Of those that a mesh axis runs over, the one named last changes fastest.
Arguments:
- grad_values: bfloat16 [1, 32, 1, 128, 12288], P('node', 'group', 'fsdp'), may hold values from -6 to 6
- grad_scales: bfloat16 [1, 32, 1, 128, 96], P('node', 'group', 'fsdp'), may hold values from 0.5 to 4
- master: float32 [1, 128, 12288], P('fsdp', 'group'), may hold values from -6 to 6
- first_moment: bfloat16 [1, 128, 12288], P('fsdp', 'group'), may hold values from -1 to 1
- first_scale: float32 [1, 128, 96], P('fsdp', 'group'), may hold values from 0.5 to 2
- second_moment: bfloat16 [1, 128, 12288], P('fsdp', 'group'), may hold values from 0.049804688 to 1
- second_scale: float32 [1, 128, 96], P('fsdp', 'group'), may hold values from 10 to 100
Outputs:
- new_master: float32 [1, 128, 12288], P('fsdp', 'group')
- new_first: bfloat16 [1, 128, 12288], P('fsdp', 'group')
- new_first_scale: float32 [1, 128, 96], P('fsdp', 'group')
- new_second: bfloat16 [1, 128, 12288], P('fsdp', 'group')
- new_second_scale: float32 [1, 128, 96], P('fsdp', 'group')
- weights: bfloat16 [1, 128, 12288], P('fsdp')
- transposed: bfloat16 [1, 12288, 128], P('fsdp')
All inputs are finite; a program needn't handle non-finite values. Where the computation divides by a largest or mean magnitude, that divisor is 1e-20 or more.
Results may differ from a plain program's by a relative error of at most 0.001.
Values may be sent and summed in bfloat16 or wider, within the bound.
A program may use at most 128 MiB of HBM per device.

v0:
```python
import jax
import jax.numpy as jnp
from jax import lax
from jax.sharding import PartitionSpec as P

BLOCK = 128


beta_one = 0.9
beta_two = 0.95
rate = 0.02
adam_eps = 1e-08
scale_eps = 1e-06
corr_one = 1.0 - 0.9**10
corr_two = 1.0 - 0.95**10


def expand(values, scales):
    shape = values.shape
    blocks = values.astype(jnp.float32).reshape(shape[:-1] + (shape[-1] // BLOCK, BLOCK))
    return (blocks * scales.astype(jnp.float32)[..., None]).reshape(shape)


def quantize(values, signed):
    shape = values.shape
    blocks = values.reshape(shape[:-1] + (shape[-1] // BLOCK, BLOCK))
    if signed:
        peak = jnp.max(jnp.abs(blocks), axis=-1) + scale_eps
    else:
        peak = jnp.max(blocks, axis=-1) + scale_eps
    coded = (blocks / peak[..., None]).astype(jnp.bfloat16).reshape(shape)
    return (coded, peak)


def adam_step(gradient, master, first_moment, first_scale, second_moment, second_scale):
    first = beta_one * expand(first_moment, first_scale) + (1.0 - beta_one) * gradient
    second = beta_two * expand(second_moment, second_scale) + (1.0 - beta_two) * gradient * gradient
    direction = first / corr_one / (jnp.sqrt(second / corr_two) + adam_eps)
    updated = master - rate * direction
    first_coded, first_peak = quantize(first, True)
    second_coded, second_peak = quantize(second, False)
    return (
        updated,
        first_coded,
        first_peak,
        second_coded,
        second_peak,
        updated.astype(jnp.bfloat16),
    )


def on_device(
    grad_values, grad_scales, master, first_moment, first_scale, second_moment, second_scale
):
    arrived, arrived_scales = (
        lax.all_to_all(grad_values, "group", split_axis=3, concat_axis=1, tiled=True),
        lax.all_to_all(grad_scales, "group", split_axis=3, concat_axis=1, tiled=True),
    )
    partial_sum = jnp.sum(expand(arrived, arrived_scales), axis=1)
    partial_sum = partial_sum.reshape(master.shape)
    gradient = lax.psum(partial_sum, "node")
    result = adam_step(gradient, master, first_moment, first_scale, second_moment, second_scale)
    updated, first_coded, first_peak, second_coded, second_peak, low_weights = result
    weights = lax.all_gather(low_weights, "group", axis=1, tiled=True)
    transposed = jnp.swapaxes(weights, 1, 2)
    return (updated, first_coded, first_peak, second_coded, second_peak, weights, transposed)


def solution(mesh):
    placed = (
        P("node", "group", "fsdp", None, None),
        P("node", "group", "fsdp", None, None),
        P("fsdp", "group", None),
        P("fsdp", "group", None),
        P("fsdp", "group", None),
        P("fsdp", "group", None),
        P("fsdp", "group", None),
    )
    return jax.shard_map(
        on_device,
        mesh=mesh,
        in_specs=placed,
        out_specs=(
            P("fsdp", "group", None),
            P("fsdp", "group", None),
            P("fsdp", "group", None),
            P("fsdp", "group", None),
            P("fsdp", "group", None),
            P("fsdp", None, None),
            P("fsdp", None, None),
        ),
        check_vma=False,
    )
```

profile of v0, /device:TPU:0, one launch (start us, length us, event | category | flops | bytes accessed | tf_op | source)
XLA Modules:
  0.0 247.5 jit_solution(14616756571123671398)
XLA Ops:
  7.2 0.9 copy.20
  8.0 0.5 broadcast.98
  8.5 0.8 reduce.6
  9.4 0.7 reshape.211
  10.1 7.3 %all-to-all-start.1 = ((bf16[32,2,192]{2,1,0:T(2,128)(2,1)}), bf16[32,2,192]{2,1,0:T(2,128)(2,1)S(1)}, u32[]{:S(2)}, u32[]{:S(2)}) async-start(bf16[32,2,192]{2,1,0:T(2,128)(2,1)} %reshape.211), calls=%async_computation.1 | async-start | bytes 65536 | tf_op jit(solution)/shard_map/all_to_all | solution.py:57
  17.4 8.6 %copy.48 = bf16[1,1,1,128,12288]{4,2,1,0,3:T(2,128)(2,1)} copy(bf16[1,1,1,128,12288]{4,3,2,1,0:T(8,128)(2,1)} %param.7) | data formatting | bytes 6291456 | tf_op args[0]
  26.0 19.0 %reduce.5 = bf16[128,12288]{1,0:T(8,128)(2,1)S(1)} reduce(bf16[128,1,1,1,12288]{4,3,2,1,0:T(2,128)(2,1)} %bitcast.26, bf16[]{:T(256)} %broadcast.98), dimensions={1,2,3}, to_apply=%bitcast.23.reduce_sub_computation | reduce | bytes 6291458
  45.0 3.6 %reshape.209 = bf16[32,2,24576]{2,1,0:T(2,128)(2,1)} reshape(bf16[128,12288]{1,0:T(8,128)(2,1)S(1)} %reduce.5) | data formatting | bytes 6291456
  48.6 5.8 %all-to-all-start = ((bf16[32,2,24576]{2,1,0:T(2,128)(2,1)}), bf16[32,2,24576]{2,1,0:T(2,128)(2,1)S(1)}, u32[]{:S(2)}, u32[]{:S(2)}) async-start(bf16[32,2,24576]{2,1,0:T(2,128)(2,1)} %reshape.209), calls=%async_computation | async-start | bytes 6291456 | tf_op jit(solution)/shard_map/all_to_all | solution.py:56
  54.5 0.2 all-gather.2.cloned.1.call-start
  54.8 71.1 %all-to-all-done = bf16[32,2,24576]{2,1,0:T(2,128)(2,1)S(1)} async-done(((bf16[32,2,24576]{2,1,0:T(2,128)(2,1)}), bf16[32,2,24576]{2,1,0:T(2,128)(2,1)S(1)}, u32[]{:S(2)}, u32[]{:S(2)}) %all-to-all-start) | async-done | bytes 3145760 | tf_op jit(solution)/shard_map/all_to_all | solution.py:56
  125.9 12.4 %reshape.210 = bf16[128,1,1,1,12288]{4,3,2,1,0:T(2,128)(2,1)} reshape(bf16[32,2,24576]{2,1,0:T(2,128)(2,1)S(1)} %all-to-all-done) | data formatting | bytes 6291456
  138.3 7.8 %bitcast_convert_fusion = f32[1,1,1,128,12288]{4,2,1,0,3:T(1,128)S(1)} fusion(bf16[128,1,1,1,12288]{4,3,2,1,0:T(2,128)(2,1)} %reshape.210), kind=kLoop, calls=%fused_computation.19 | loop fusion | flops 1572864 | bytes 9437184 | tf_op jit(solution)/shard_map/convert_element_type | solution.py:20
  146.1 2.0 multiply_reduce_fusion
  148.4 2.1 fusion.8
  150.5 0.8 copy.24
  151.8 0.6 fusion.7
  152.4 0.6 fusion.6
  153.2 0.4 divide_convert_fusion
  153.6 0.8 copy.25
  154.4 0.8 copy.26
  155.2 64.3 %all-gather.2.cloned.1.call-done = bf16[1,128,12288]{2,0,1:T(2,128)(2,1)} async-done(((bf16[1,4,12288]{2,0,1:T(2,128)(2,1)}), bf16[1,128,12288]{2,0,1:T(2,128)(2,1)}) %all-gather.2.cloned.1.call-update) | async-done | bytes 3145744 | tf_op jit(solution)/shard_map/all_gather | solution.py:64
  219.5 13.4 %copy.28 = bf16[1,12288,128]{2,1,0:T(8,128)(2,1)} copy(bf16[1,12288,128]{1,0,2:T(2,128)(2,1)} %bitcast.24) | data formatting | bytes 6291456
  232.8 7.8 %copy.27 = bf16[1,128,12288]{2,1,0:T(8,128)(2,1)} copy(bf16[1,128,12288]{2,0,1:T(2,128)(2,1)} %all-gather.2.cloned.1.call-done) | data formatting | bytes 6291456
  (22 shorter events, 1.1 us)
Async XLA Ops:
  10.1 38.5 %all-to-all-start.1 = ((bf16[32,2,192]{2,1,0:T(2,128)(2,1)}), bf16[32,2,192]{2,1,0:T(2,128)(2,1)S(1)}, u32[]{:S(2)}, u32[]{:S(2)}) async-start(bf16[32,2,192]{2,1,0:T(2,128)(2,1)} %reshape.211), calls=%async_computation.1 | async-start | bytes 65536 | tf_op jit(solution)/shard_map/all_to_all | solution.py:57
  48.6 77.3 %all-to-all-start = ((bf16[32,2,24576]{2,1,0:T(2,128)(2,1)}), bf16[32,2,24576]{2,1,0:T(2,128)(2,1)S(1)}, u32[]{:S(2)}, u32[]{:S(2)}) async-start(bf16[32,2,24576]{2,1,0:T(2,128)(2,1)} %reshape.209), calls=%async_computation | async-start | bytes 6291456 | tf_op jit(solution)/shard_map/all_to_all | solution.py:56
  54.5 165.0 %all-gather.2.cloned.1.call-start = ((), (), s32[]{:S(2)}) async-start(), calls=%async_computation.2 | async-start | bytes 6488064 | tf_op jit(solution)/shard_map/all_gather | solution.py:64
  146.1 2.0 copy-start.3
  146.1 2.1 copy-start.4
  146.1 2.2 copy-start
  146.1 2.2 copy-start.1
  146.1 2.2 copy-start.2
Sparse Core Ops, SparseCore 0:
  150.6 68.8 all-gather.1
where the time goes:
time: 248 us
  waiting for transfers between devices  135 us (54%)
  local copies, waits for them, and re-layouts  50.8 us (20%)
  other arithmetic  33.7 us (14%)
  between operations  14.2 us (6%)
  starting transfers between devices  13.4 us (5%)
    all_to_all x1, waiting for transfers between devices, on_device(): lax.all_to_all(grad_values, 'group', split_axis=3, concat_axis=1, tiled=T...  71.1 us
    all_gather x1, waiting for transfers between devices, on_device(): weights = lax.all_gather(low_weights, 'group', axis=1, tiled=True)  64.3 us
    unnamed x22, local copies, waits for them, and re-layouts  50.4 us
    unnamed x2, other arithmetic  19.8 us
    convert_element_type x1, other arithmetic, expand(): values.astype(jnp.float32).reshape(shape[:-1] + (shape[-1] // BLOCK, BLOCK))  7.77 us
    all_to_all x1, starting transfers between devices, on_device(): lax.all_to_all(grad_scales, 'group', split_axis=3, concat_axis=1, tiled=T...  7.3 us
    all_to_all x1, starting transfers between devices, on_device(): lax.all_to_all(grad_values, 'group', split_axis=3, concat_axis=1, tiled=T...  5.83 us
  transfers between devices with their start and end apart: 3, of which 2 were waited for; matrix products, arithmetic and copies ran while one was open for 15% of the time, Pallas kernels for 0%

commit v1 on v0

--- a/solution.py
+++ b/solution.py
@@ -1,10 +1,16 @@
+import functools
+
 import jax
 import jax.numpy as jnp
 from jax import lax
+from jax.experimental import pallas as pl
+from jax.experimental.pallas import tpu as pltpu
 from jax.sharding import PartitionSpec as P
 
 BLOCK = 128
-
+CHUNKS = 4
+GROUPS = 2
+TILE = 16
 
 beta_one = 0.9
 beta_two = 0.95
@@ -14,21 +20,432 @@
 corr_one = 1.0 - 0.9**10
 corr_two = 1.0 - 0.95**10
 
+f32 = jnp.float32
+bf16 = jnp.bfloat16
+
+
+def exchange_kernel(
+    grad, gscale, master, fm, fs, sm, ss,
+    comm, new_master, new_first, new_fs, new_second, new_ss,
+    own, sib, sc_sib, sh_own, sh_sib, part, rx1, rx2, acc, rx3, gfull, fbase, sbase, slotf, slot,
+    own_sem, sc_sem, sib_sem, p1_sem, p2_sem, z_sem, g_sem,
+    az_sem, ax_sem, ay_sem, fx_sem, fy_sem, as_sem, loc_sem,
+):
+    half = grad.shape[1] // 2
+    w = half // CHUNKS
+    nb = w // BLOCK
+    hb = half // BLOCK
+    me = lax.axis_index("group")
+    c = lax.rem(me, 2)
+    x = lax.rem(me // 2, 2)
+    y = lax.rem(me // 4, 2)
+    z = me // 8
+
+    def index(zz, yy, xx, cc):
+        return zz * 8 + yy * 4 + xx * 2 + cc
+
+    sibling = index(z, y, x, 1 - c)
+    xn = index(z, y, 1 - x, c)
+    yn = index(z, 1 - y, x, c)
+    z_up = [lax.rem(z + d, 4) for d in range(4)]
+    z_from = [lax.rem(z + 4 - d, 4) for d in range(4)]
+    zn = [index(z_up[d], y, x, c) for d in range(4)]
+
+    def remote(src, dst, sems, at, to):
+        return pltpu.make_async_remote_copy(
+            src_ref=src,
+            dst_ref=dst,
+            send_sem=sems.at[(0,) + at],
+            recv_sem=sems.at[(1,) + at],
+            device_id={"group": to},
+            device_id_type=pl.DeviceIdType.MESH,
+        )
+
+    sent = []
+
+    def send(*args):
+        copy = remote(*args)
+        copy.start()
+        sent.append(copy)
+        return copy
+
+    barrier = pltpu.get_barrier_semaphore()
+    partners = [sibling, xn, yn] + zn[1:]
+    for to in partners:
+        pl.semaphore_signal(
+            barrier, inc=1, device_id={"group": to}, device_id_type=pl.DeviceIdType.MESH
+        )
+    pl.semaphore_wait(barrier, len(partners))
+
+    scale_copy = send(gscale, sc_sib, sc_sem, (0,), sibling)
+    sib_copies, own_copies = [], []
+    for k in range(CHUNKS):
+        there = pl.multiple_of((1 - c) * half + k * w, BLOCK)
+        here = pl.multiple_of(c * half + k * w, BLOCK)
+        sib_copies.append(send(grad.at[:, pl.ds(there, w)], sib.at[k], sib_sem, (k,), sibling))
+        copy = pltpu.make_async_copy(grad.at[:, pl.ds(here, w)], own.at[k], own_sem.at[k])
+        copy.start()
+        own_copies.append(copy)
+
+    def half_scales(ref):
+        values = ref[...].astype(f32)
+        return jnp.where(c == 0, values[:, :hb], values[:, hb:])
+
+    sh_own[...] = half_scales(gscale)
+    scale_copy.wait_recv()
+    sh_sib[...] = half_scales(sc_sib)
+
+    def order(k):
+        return (x, y, xn, yn) if k % 2 == 0 else (y, x, yn, xn)
+
+    p1, p2, gc = {}, {}, {}
+
+    def core_sum(k):
+        own_copies[k].wait()
+        sib_copies[k].wait_recv()
+
+        def body(i, carry):
+            rows = pl.ds(pl.multiple_of(i * 16, 16), 16)
+            so, sb = sh_own[rows, :], sh_sib[rows, :]
+            zz, yy = i // 2, lax.rem(i, 2)
+            for b in range(nb):
+                j = k * nb + b
+                cols = pl.ds(b * BLOCK, BLOCK)
+                v = own[k, rows, cols].astype(f32) * so[:, j : j + 1]
+                v += sib[k, rows, cols].astype(f32) * sb[:, j : j + 1]
+                for xx in range(2):
+                    one, two = (xx, yy) if k % 2 == 0 else (yy, xx)
+                    part[k, one, two, zz, :, cols] = v[8 * xx : 8 * xx + 8]
+            return carry
+
+        lax.fori_loop(0, 8, body, 0)
+        a, _, an, _ = order(k)
+        p1[k] = send(part.at[k, 1 - a], rx1.at[k], p1_sem, (k,), an)
+
+    def base(k):
+        for h in range(2):
+            for b in range(nb):
+                j = h * hb + k * nb + b
+                cols = pl.ds(j * BLOCK, BLOCK)
+                fbase[:, cols] = beta_one * (fm[:, cols].astype(f32) * fs[:, j : j + 1])
+                sbase[:, cols] = beta_two * (sm[:, cols].astype(f32) * ss[:, j : j + 1])
+
+    def first_axis(k):
+        a, b, _, bn = order(k)
+        p1[k].wait_recv()
+        for zz in range(4):
+            part[k, a, 1 - b, zz] = part[k, a, 1 - b, zz] + rx1[k, 1 - b, zz]
+        p2[k] = send(part.at[k, a, 1 - b], rx2.at[k], p2_sem, (k,), bn)
+
+    def second_axis(k):
+        a, b, _, _ = order(k)
+        p2[k].wait_recv()
+        for zz in range(4):
+            acc[k, zz] = part[k, a, b, zz] + rx1[k, b, zz] + rx2[k, zz]
+        for d in range(1, 4):
+            send(acc.at[k, z_up[d]], rx3.at[k, d], z_sem, (k, d), zn[d])
+
+    def along_z(k):
+        total = acc[k, z]
+        for d in range(1, 4):
+            remote(acc.at[k, z_up[d]], rx3.at[k, d], z_sem, (k, d), zn[d]).wait_recv()
+            total = total + rx3[k, d]
+        gfull[c, k] = total
+        gc[k] = send(gfull.at[c, k], gfull.at[c, k], g_sem, (k,), sibling)
+
+    def adam(k):
+        remote(gfull.at[1 - c, k], gfull.at[1 - c, k], g_sem, (k,), sibling).wait_recv()
+        for h in range(2):
+            cols = pl.ds(h * half + k * w, w)
+            v = gfull[h, k]
+            g = jnp.where(c == 0, v[0:4], v[4:8])
+            first = fbase[:, cols] + (1.0 - beta_one) * g
+            second = sbase[:, cols] + (1.0 - beta_two) * g * g
+            fbase[:, cols] = first
+            sbase[:, cols] = second
+            direction = first / corr_one / (jnp.sqrt(second / corr_two) + adam_eps)
+            updated = master[:, cols] - rate * direction
+            new_master[:, cols] = updated
+            for q in range(2):
+                r = 4 * (2 * h + q)
+                slotf[r : r + 4, k * (w // 2) : (k + 1) * (w // 2)] = updated[
+                    :, q * (w // 2) : (q + 1) * (w // 2)
+                ]
+
+    def quantize(k):
+        for h in range(2):
+            for b in range(nb):
+                j = h * hb + k * nb + b
+                cols = pl.ds(j * BLOCK, BLOCK)
+                first, second = fbase[:, cols], sbase[:, cols]
+                peak = jnp.max(jnp.abs(first), axis=1, keepdims=True) + scale_eps
+                new_fs[:, j : j + 1] = peak
+                new_first[:, cols] = (first / peak).astype(bf16)
+                peak = jnp.max(second, axis=1, keepdims=True) + scale_eps
+                new_ss[:, j : j + 1] = peak
+                new_second[:, cols] = (second / peak).astype(bf16)
+
+    per = CHUNKS // GROUPS
+    wide = per * (w // 2)
+    locals_ = []
+
+    def place(e, zz, yy, xx, lo=0, width=wide):
+        row = pl.multiple_of(index(zz, yy, xx, c) * TILE, TILE)
+        return comm.at[pl.ds(row, TILE), pl.ds(e * wide + lo, width)]
+
+    def gather_own(e):
+        cols = pl.ds(e * wide, wide)
+        slot[:, cols] = slotf[:, cols].astype(bf16)
+        src, dst = slot.at[:, cols], place(e, z, y, x)
+        for d in range(1, 4):
+            send(src, dst, az_sem, (e, d), zn[d])
+        send(src, dst, ax_sem, (e, 0), xn)
+        send(src, dst, ay_sem, (e, 0), yn)
+        send(src, dst, as_sem, (e, 0), sibling)
+        copy = pltpu.make_async_copy(src, dst, loc_sem.at[e])
+        copy.start()
+        locals_.append(copy)
+
+    def gather_z(e):
+        for d in range(1, 4):
+            ref = place(e, z_from[d], y, x)
+            remote(ref, ref, az_sem, (e, d), zn[d]).wait_recv()
+            send(ref, ref, ax_sem, (e, d), xn)
+            send(ref, ref, ay_sem, (e, d), yn)
+            send(ref, ref, as_sem, (e, d), sibling)
+
+    def gather_xy(e):
+        for d in range(4):
+            ref = place(e, z_from[d], y, 1 - x)
+            remote(ref, ref, ax_sem, (e, d), xn).wait_recv()
+            right = place(e, z_from[d], y, 1 - x, wide // 2, wide // 2)
+            send(right, right, fy_sem, (e, d), yn)
+            send(ref, ref, as_sem, (e, 4 + d), sibling)
+            ref = place(e, z_from[d], 1 - y, x)
+            remote(ref, ref, ay_sem, (e, d), yn).wait_recv()
+            left = place(e, z_from[d], 1 - y, x, 0, wide // 2)
+            send(left, left, fx_sem, (e, d), xn)
+            send(ref, ref, as_sem, (e, 8 + d), sibling)
+
+    def gather_far(e):
+        for d in range(4):
+            ref = place(e, z_from[d], 1 - y, 1 - x)
+            left = place(e, z_from[d], 1 - y, 1 - x, 0, wide // 2)
+            right = place(e, z_from[d], 1 - y, 1 - x, wide // 2, wide // 2)
+            remote(left, left, fx_sem, (e, d), xn).wait_recv()
+            remote(right, right, fy_sem, (e, d), yn).wait_recv()
+            send(ref, ref, as_sem, (e, 12 + d), sibling)
+
+    def gather_end(e):
+        for q in range(4):
+            for d in range(4):
+                yy = 1 - y if q >= 2 else y
+                xx = 1 - x if q % 2 == 1 else x
+                row = pl.multiple_of(index(z_from[d], yy, xx, 1 - c) * TILE, TILE)
+                ref = comm.at[pl.ds(row, TILE), pl.ds(e * wide, wide)]
+                remote(ref, ref, as_sem, (e, 4 * q + d), sibling).wait_recv()
+
+    for k in range(CHUNKS):
+        core_sum(k)
+    for k in range(CHUNKS):
+        base(k)
+    for k in range(CHUNKS):
+        first_axis(k)
+    for k in range(CHUNKS):
+        second_axis(k)
+    for e in range(GROUPS):
+        ks = range(e * per, (e + 1) * per)
+        for k in ks:
+            along_z(k)
+        for k in ks:
+            adam(k)
+        gather_own(e)
+        if e < GROUPS - 1:
+            for k in ks:
+                quantize(k)
+    for e in range(GROUPS):
+        gather_z(e)
+    for k in range((GROUPS - 1) * per, CHUNKS):
+        quantize(k)
+    for e in range(GROUPS):
+        gather_xy(e)
+    for e in range(GROUPS):
+        gather_far(e)
+    for e in range(GROUPS):
+        gather_end(e)
+    for copy in sent:
+        copy.wait_send()
+    for copy in locals_:
+        copy.wait()
+
+
+def exchange(grad, gscale, master, fm, fs, sm, ss):
+    rows, d = grad.shape
+    own_rows = master.shape[0]
+    w = d // 2 // CHUNKS
+    K, G = CHUNKS, GROUPS
+    vmem = pl.BlockSpec(memory_space=pltpu.VMEM)
+    dma = pltpu.SemaphoreType.DMA
+    return pl.pallas_call(
+        exchange_kernel,
+        out_shape=(
+            jax.ShapeDtypeStruct((rows * 4, d // 4), bf16),
+            jax.ShapeDtypeStruct(master.shape, f32),
+            jax.ShapeDtypeStruct(fm.shape, bf16),
+            jax.ShapeDtypeStruct(fs.shape, f32),
+            jax.ShapeDtypeStruct(sm.shape, bf16),
+            jax.ShapeDtypeStruct(ss.shape, f32),
+        ),
+        in_specs=[pl.BlockSpec(memory_space=pl.ANY)] + [vmem] * 6,
+        out_specs=(pl.BlockSpec(memory_space=pl.ANY),) + (vmem,) * 5,
+        scratch_shapes=[
+            pltpu.VMEM((K, rows, w), bf16),
+            pltpu.VMEM((K, rows, w), bf16),
+            pltpu.VMEM(gscale.shape, bf16),
+            pltpu.VMEM((rows, gscale.shape[1] // 2), f32),
+            pltpu.VMEM((rows, gscale.shape[1] // 2), f32),
+            pltpu.VMEM((K, 2, 2, 4, 8, w), f32),
+            pltpu.VMEM((K, 2, 4, 8, w), f32),
+            pltpu.VMEM((K, 4, 8, w), f32),
+            pltpu.VMEM((K, 4, 8, w), f32),
+            pltpu.VMEM((K, 4, 8, w), f32),
+            pltpu.VMEM((2, K, 8, w), f32),
+            pltpu.VMEM((own_rows, d), f32),
+            pltpu.VMEM((own_rows, d), f32),
+            pltpu.VMEM((TILE, d // 4), f32),
+            pltpu.VMEM((TILE, d // 4), bf16),
+            dma((K,)),
+            dma((2, 1)),
+            dma((2, K)),
+            dma((2, K)),
+            dma((2, K)),
+            dma((2, K, 4)),
+            dma((2, K)),
+            dma((2, G, 4)),
+            dma((2, G, 4)),
+            dma((2, G, 4)),
+            dma((2, G, 4)),
+            dma((2, G, 4)),
+            dma((2, G, 16)),
+            dma((G,)),
+        ],
+        compiler_params=pltpu.CompilerParams(
+            collective_id=0, has_side_effects=True, vmem_limit_bytes=40 * 1024 * 1024
+        ),
+        cost_estimate=pl.CostEstimate(
+            flops=8 * rows * d, bytes_accessed=8 * rows * d, transcendentals=own_rows * d
+        ),
+        name="exchange",
+    )(grad, gscale, master, fm, fs, sm, ss)
+
+
+def assemble_kernel(comm, *refs):
+    smalls, (weights, transposed), copied = refs[:5], refs[5:7], refs[7:12]
+    sem = refs[12]
+    t = pl.program_id(0) * 4 + pl.program_id(1)
+    last = pl.num_programs(0) * 4 - 1
+    copies = [pltpu.make_async_copy(a, b, sem.at[i]) for i, (a, b) in enumerate(zip(smalls, copied))]
+
+    @pl.when(t == 0)
+    def _():
+        for copy in copies:
+            copy.start()
+
+    rows, cols = weights.shape
+    kk = pl.program_id(1)
+    row = lax.broadcasted_iota(jnp.int32, (rows, rows * 4), 0)
+    col = lax.broadcasted_iota(jnp.int32, (rows, rows * 4), 1)
+    wanted = (row // 4) * TILE + 4 * kk + lax.rem(row, 4)
+    pick = jnp.where(col == wanted, 1.0, 0.0).astype(bf16)
+    w = jnp.dot(pick, comm[...], preferred_element_type=f32).astype(bf16)
+    weights[...] = w
+    step = 256
+    eye = jnp.where(
+        lax.broadcasted_iota(jnp.int32, (step, step), 0)
+        == lax.broadcasted_iota(jnp.int32, (step, step), 1),
+        1.0,
+        0.0,
+    ).astype(bf16)
+    for i in range(cols // step):
+        turned = lax.dot_general(
+            eye,
+            w[:, i * step : (i + 1) * step],
+            (((1,), (1,)), ((), ())),
+            preferred_element_type=f32,
+        )
+        transposed[i * step : (i + 1) * step, :] = turned.astype(bf16)
+
+    @pl.when(t == last)
+    def _():
+        for copy in copies:
+            copy.wait()
+
+
+def assemble(comm, smalls):
+    rows = comm.shape[0] // 4
+    d = comm.shape[1] * 4
+    cols = d // 4 // CHUNKS
+    anywhere = pl.BlockSpec(memory_space=pl.ANY)
+
+    def column(k, kk):
+        return (kk // 2) * (2 * CHUNKS) + 2 * k + lax.rem(kk, 2)
+
+    return pl.pallas_call(
+        assemble_kernel,
+        grid=(CHUNKS, 4),
+        out_shape=(
+            jax.ShapeDtypeStruct((rows, d), bf16),
+            jax.ShapeDtypeStruct((d, rows), bf16),
+        )
+        + tuple(jax.ShapeDtypeStruct(s.shape, s.dtype) for s in smalls),
+        in_specs=[pl.BlockSpec((rows * 4, cols), lambda k, kk: (0, k))] + [anywhere] * 5,
+        out_specs=(
+            pl.BlockSpec((rows, cols), lambda k, kk: (0, column(k, kk))),
+            pl.BlockSpec((cols, rows), lambda k, kk: (column(k, kk), 0)),
+        )
+        + (anywhere,) * 5,
+        scratch_shapes=[pltpu.SemaphoreType.DMA((5,))],
+        compiler_params=pltpu.CompilerParams(
+            vmem_limit_bytes=32 * 1024 * 1024,
+            dimension_semantics=("arbitrary", "arbitrary"),
+        ),
+        name="assemble",
+    )(comm, *smalls)
+
+
+def fused_on_device(
+    grad_values, grad_scales, master, first_moment, first_scale, second_moment, second_scale
+):
+    def flat(array):
+        return array.reshape(array.shape[-2:])
+
+    comm, *smalls = exchange(
+        flat(grad_values),
+        flat(grad_scales),
+        flat(master),
+        flat(first_moment),
+        flat(first_scale),
+        flat(second_moment),
+        flat(second_scale),
+    )
+    weights, transposed, *smalls = assemble(comm, smalls)
+    return tuple(array[None] for array in (*smalls, weights, transposed))
+
 
 def expand(values, scales):
     shape = values.shape
-    blocks = values.astype(jnp.float32).reshape(shape[:-1] + (shape[-1] // BLOCK, BLOCK))
-    return (blocks * scales.astype(jnp.float32)[..., None]).reshape(shape)
-
-
-def quantize(values, signed):
+    blocks = values.astype(f32).reshape(shape[:-1] + (shape[-1] // BLOCK, BLOCK))
+    return (blocks * scales.astype(f32)[..., None]).reshape(shape)
+
+
+def quantize_blocks(values, signed):
     shape = values.shape
     blocks = values.reshape(shape[:-1] + (shape[-1] // BLOCK, BLOCK))
     if signed:
         peak = jnp.max(jnp.abs(blocks), axis=-1) + scale_eps
     else:
         peak = jnp.max(blocks, axis=-1) + scale_eps
-    coded = (blocks / peak[..., None]).astype(jnp.bfloat16).reshape(shape)
+    coded = (blocks / peak[..., None]).astype(bf16).reshape(shape)
     return (coded, peak)
 
 
@@ -37,16 +454,9 @@
     second = beta_two * expand(second_moment, second_scale) + (1.0 - beta_two) * gradient * gradient
     direction = first / corr_one / (jnp.sqrt(second / corr_two) + adam_eps)
     updated = master - rate * direction
-    first_coded, first_peak = quantize(first, True)
-    second_coded, second_peak = quantize(second, False)
-    return (
-        updated,
-        first_coded,
-        first_peak,
-        second_coded,
-        second_peak,
-        updated.astype(jnp.bfloat16),
-    )
+    first_coded, first_peak = quantize_blocks(first, True)
+    second_coded, second_peak = quantize_blocks(second, False)
+    return (updated, first_coded, first_peak, second_coded, second_peak, updated.astype(bf16))
 
 
 def on_device(
@@ -76,8 +486,9 @@
         P("fsdp", "group", None),
         P("fsdp", "group", None),
     )
+    fused = mesh.shape["node"] == 1 and mesh.shape["group"] == 32
     return jax.shard_map(
-        on_device,
+        fused_on_device if fused else on_device,
         mesh=mesh,
         in_specs=placed,
         out_specs=(

time: 248 us -> 89.6 us (0.36)
  waiting for transfers between devices: 135 us -> 0 us
  Pallas kernels: 0 us -> 81.7 us
  local copies, waits for them, and re-layouts: 50.8 us -> 6.81 us
  other arithmetic: 33.7 us -> 0 us
  between operations: 14.2 us -> 0.66 us
  starting transfers between devices: 13.4 us -> 0 us
    pallas_call x0 -> x2, Pallas kernels: none -> 81.7 us  [the longest x1 71 us: exchange(): pl.pallas_call(exchange_kernel, out_shape=(jax.ShapeDtypeStruct((rows * 4...]
    all_to_all x2 -> x0, waiting for transfers between devices: 71.1 us -> none  [the longest x1 71.1 us: on_device(): lax.all_to_all(grad_values, 'group', split_axis=3, concat_axis=1, tiled=T...]
    all_gather x1 -> x0, waiting for transfers between devices: 64.3 us -> none  [on_device(): weights = lax.all_gather(low_weights, 'group', axis=1, tiled=True)]
    unnamed x22 -> x13, local copies, waits for them, and re-layouts: 50.4 us -> 6.81 us
    unnamed x2 -> x0, other arithmetic: 19.8 us -> none
    all_to_all x2 -> x0, starting transfers between devices: 13.1 us -> none  [the longest x1 7.3 us: on_device(): lax.all_to_all(grad_scales, 'group', split_axis=3, concat_axis=1, tiled=T...]
    convert_element_type x4 -> x0, other arithmetic: 10.3 us -> none  [the longest x1 7.77 us: expand(): values.astype(jnp.float32).reshape(shape[:-1] + (shape[-1] // BLOCK, BLOCK))]
  transfers between devices with their start and end apart: 3 -> 0, of which waited for: 2 -> 0; matrix products, arithmetic and copies ran while one was open for 15% -> 0% of each run, Pallas kernels for 0% -> 0%
where the time goes in v1:
time: 89.6 us; the launch traced here: 89.2 us
  Pallas kernels  81.7 us (91%)
  local copies, waits for them, and re-layouts  6.81 us (8%)
    pallas_call x1, Pallas kernels, exchange(): pl.pallas_call(exchange_kernel, out_shape=(jax.ShapeDtypeStruct((rows * 4...  71 us
    pallas_call x1, Pallas kernels, assemble(): pl.pallas_call(assemble_kernel, grid=(CHUNKS, 4), out_shape=(jax.ShapeDty...  10.7 us
    unnamed x13, local copies, waits for them, and re-layouts  6.81 us

profile of v1, /device:TPU:0, one launch (start us, length us, event | category | flops | bytes accessed | tf_op | source)
XLA Modules:
  0.0 89.2 jit_solution(15497485593413652493)
XLA Ops:
  0.6 0.8 copy.14
  1.5 0.0 copy-start
  1.5 1.9 %copy-done = bf16[1,1,1,128,12288]{4,3,2,1,0:T(8,128)(2,1)S(1)} copy-done((bf16[1,1,1,128,12288]{4,3,2,1,0:T(8,128)(2,1)S(1)}, bf16[1,1,1,128,12288]{4,3,2,1,0:T(8,128)(2,1)}, u32[]{:S(2)}) %copy-start) | copy-done | bytes 3145752
  3.4 0.0 copy-start.1
  3.4 0.9 %copy-done.1 = f32[1,4,12288]{2,1,0:T(4,128)S(1)} copy-done((f32[1,4,12288]{2,1,0:T(4,128)S(1)}, f32[1,4,12288]{2,1,0:T(4,128)}, u32[]{:S(2)}) %copy-start.1) | copy-done | bytes 196632
  4.3 0.0 copy-start.2
  4.3 0.9 copy-done.2
  5.2 0.0 copy-start.3
  5.2 0.9 copy-done.3
  6.1 0.0 copy-start.4
  6.1 0.7 copy-done.4
  6.8 0.0 copy-start.5
  6.8 0.7 copy-done.5
  7.5 71.0 %exchange.1 = (bf16[512,3072]{1,0:T(8,128)(2,1)S(1)}, f32[4,12288]{1,0:T(4,128)S(1)}, bf16[4,12288]{1,0:T(4,128)(2,1)S(1)}, f32[4,96]{1,0:T(4,128)S(1)}, bf16[4,...) custom-call(bf16[128,12288]{1,0:T(8,128)(2,1)S(1)} %bitcast.14, bf16[128,96]{1,0:T(8,128)(2,1)S(1)} %bitcast.16, ...), custom_call_target="tpu_custom_call" | custom-call | flops 12582912 | bytes 12582912 | tf_op jit(solution)/shard_map/exchange/pallas_call | solution.py:289
  78.5 10.7 %assemble.1 = (bf16[128,12288]{1,0:T(8,128)(2,1)}, bf16[12288,128]{1,0:T(8,128)(2,1)}, f32[4,12288]{1,0:T(4,128)}, bf16[4,12288]{1,0:T(4,128)(2,1)}, f32[4,96]{1...) custom-call(bf16[512,3072]{1,0:T(8,128)(2,1)S(1)} %get-tuple-element.20.comm, ...), custom_call_target="tpu_custom_call" | custom-call | tf_op jit(solution)/shard_map/assemble/pallas_call | solution.py:393
Async XLA Ops:
  1.5 1.9 %copy-start = (bf16[1,1,1,128,12288]{4,3,2,1,0:T(8,128)(2,1)S(1)}, bf16[1,1,1,128,12288]{4,3,2,1,0:T(8,128)(2,1)}, u32[]{:S(2)}) copy-start(bf16[1,1,1,128,12288]{4,3,2,1,0:T(8,128)(2,1)} %param.7) | copy-start | bytes 9437188
  3.4 0.9 %copy-start.1 = (f32[1,4,12288]{2,1,0:T(4,128)S(1)}, f32[1,4,12288]{2,1,0:T(4,128)}, u32[]{:S(2)}) copy-start(f32[1,4,12288]{2,1,0:T(4,128)} %param.9) | copy-start | bytes 589828
  4.3 0.9 %copy-start.2 = (bf16[1,4,12288]{2,1,0:T(4,128)(2,1)S(1)}, bf16[1,4,12288]{2,1,0:T(4,128)(2,1)}, u32[]{:S(2)}) copy-start(bf16[1,4,12288]{2,1,0:T(4,128)(2,1)} %param.10) | copy-start | bytes 294916
  5.2 0.9 %copy-start.3 = (bf16[1,4,12288]{2,1,0:T(4,128)(2,1)S(1)}, bf16[1,4,12288]{2,1,0:T(4,128)(2,1)}, u32[]{:S(2)}) copy-start(bf16[1,4,12288]{2,1,0:T(4,128)(2,1)} %param.12) | copy-start | bytes 294916
  6.1 0.7 copy-start.4
  6.8 0.7 copy-start.5

commit v2 on v1

v2 whole, which is shorter than its diff:
```python
import functools

import jax
import jax.numpy as jnp
from jax import lax
from jax.experimental import pallas as pl
from jax.experimental.pallas import tpu as pltpu
from jax.sharding import PartitionSpec as P

BLOCK = 128
CHUNKS = 8
GROUPS = 4
TILE = 16

beta_one = 0.9
beta_two = 0.95
rate = 0.02
adam_eps = 1e-08
scale_eps = 1e-06
corr_one = 1.0 - 0.9**10
corr_two = 1.0 - 0.95**10

f32 = jnp.float32
bf16 = jnp.bfloat16


def exchange_kernel(
    grad, gscale, master_in, fm_in, fs_in, sm_in, ss_in,
    comm, master_out, first_out, fs_out, second_out, ss_out,
    own, sib, sc_own, sc_sib, sh_own, sh_sib, part, rx1, rx2, acc, rx3, gfull, fbase, sbase, slotf, slot,
    master, fm, fs, sm, ss, new_master, new_first, new_fs, new_second, new_ss,
    in_sem, out_sem, own_sem, sc_sem, sib_sem, p1_sem, p2_sem, z_sem, g_sem,
    az_sem, ax_sem, ay_sem, fx_sem, fy_sem, as_sem, loc_sem,
):
    w = grad.shape[1] // 2 // CHUNKS
    nb = w // BLOCK
    me = lax.axis_index("group")
    c = lax.rem(me, 2)
    x = lax.rem(me // 2, 2)
    y = lax.rem(me // 4, 2)
    z = me // 8

    def index(zz, yy, xx, cc):
        return zz * 8 + yy * 4 + xx * 2 + cc

    sibling = index(z, y, x, 1 - c)
    xn = index(z, y, 1 - x, c)
    yn = index(z, 1 - y, x, c)
    z_up = [lax.rem(z + d, 4) for d in range(4)]
    z_from = [lax.rem(z + 4 - d, 4) for d in range(4)]
    zn = [index(z_up[d], y, x, c) for d in range(4)]

    def remote(src, dst, sems, at, to):
        return pltpu.make_async_remote_copy(
            src_ref=src,
            dst_ref=dst,
            send_sem=sems.at[(0,) + at],
            recv_sem=sems.at[(1,) + at],
            device_id={"group": to},
            device_id_type=pl.DeviceIdType.MESH,
        )

    sent = []

    def send(*args):
        copy = remote(*args)
        copy.start()
        sent.append(copy)
        return copy

    def local(src, dst, sem):
        copy = pltpu.make_async_copy(src, dst, sem)
        copy.start()
        return copy

    def columns(k, h):
        return k * 2 * w + h * w

    scale_own = local(gscale, sc_own, in_sem.at[5])
    own_copies = []
    for k in range(CHUNKS):
        here = pl.multiple_of(columns(k, c), BLOCK)
        own_copies.append(local(grad.at[:, pl.ds(here, w)], own.at[k], own_sem.at[k]))

    barrier = pltpu.get_barrier_semaphore()
    partners = [sibling, xn, yn] + zn[1:]
    for to in partners:
        pl.semaphore_signal(
            barrier, inc=1, device_id={"group": to}, device_id_type=pl.DeviceIdType.MESH
        )
    pl.semaphore_wait(barrier, len(partners))

    scale_copy = send(gscale, sc_sib, sc_sem, (0,), sibling)
    sib_copies = []
    for k in range(CHUNKS):
        there = pl.multiple_of(columns(k, 1 - c), BLOCK)
        sib_copies.append(send(grad.at[:, pl.ds(there, w)], sib.at[k], sib_sem, (k,), sibling))
    fetched = [
        local(src, dst, in_sem.at[i])
        for i, (src, dst) in enumerate(
            ((fm_in, fm), (fs_in, fs), (sm_in, sm), (ss_in, ss), (master_in, master))
        )
    ]

    def half_scales(ref, out):
        values = ref[...].astype(f32)
        for k in range(CHUNKS):
            j = 2 * k * nb
            out[:, k * nb : (k + 1) * nb] = jnp.where(
                c == 0, values[:, j : j + nb], values[:, j + nb : j + 2 * nb]
            )

    scale_own.wait()
    half_scales(sc_own, sh_own)
    scale_copy.wait_recv()
    half_scales(sc_sib, sh_sib)

    def order(k):
        return (x, y, xn, yn) if k % 2 == 0 else (y, x, yn, xn)

    p1, p2 = {}, {}

    def core_sum(k):
        own_copies[k].wait()
        sib_copies[k].wait_recv()

        def body(i, carry):
            rows = pl.ds(pl.multiple_of(i * 16, 16), 16)
            so, sb = sh_own[rows, :], sh_sib[rows, :]
            zz, yy = i // 2, lax.rem(i, 2)
            for b in range(nb):
                j = k * nb + b
                cols = pl.ds(b * BLOCK, BLOCK)
                v = own[k, rows, cols].astype(f32) * so[:, j : j + 1]
                v += sib[k, rows, cols].astype(f32) * sb[:, j : j + 1]
                for xx in range(2):
                    one, two = (xx, yy) if k % 2 == 0 else (yy, xx)
                    part[k, one, two, zz, :, cols] = v[8 * xx : 8 * xx + 8]
            return carry

        lax.fori_loop(0, 8, body, 0)
        a, _, an, _ = order(k)
        p1[k] = send(part.at[k, 1 - a], rx1.at[k], p1_sem, (k,), an)

    def base(k):
        for b in range(2 * nb):
            j = 2 * k * nb + b
            cols = pl.ds(j * BLOCK, BLOCK)
            fbase[:, cols] = beta_one * (fm[:, cols].astype(f32) * fs[:, j : j + 1])
            sbase[:, cols] = beta_two * (sm[:, cols].astype(f32) * ss[:, j : j + 1])

    def first_axis(k):
        a, b, _, bn = order(k)
        p1[k].wait_recv()
        for zz in range(4):
            part[k, a, 1 - b, zz] = part[k, a, 1 - b, zz] + rx1[k, 1 - b, zz]
        p2[k] = send(part.at[k, a, 1 - b], rx2.at[k], p2_sem, (k,), bn)

    def second_axis(k):
        a, b, _, _ = order(k)
        p2[k].wait_recv()
        for zz in range(4):
            acc[k, zz] = part[k, a, b, zz] + rx1[k, b, zz] + rx2[k, zz]
        for d in range(1, 4):
            send(acc.at[k, z_up[d]], rx3.at[k, d], z_sem, (k, d), zn[d])

    def along_z(k):
        total = acc[k, z]
        for d in range(1, 4):
            remote(acc.at[k, z_up[d]], rx3.at[k, d], z_sem, (k, d), zn[d]).wait_recv()
            total = total + rx3[k, d]
        gfull[c, k] = total
        send(gfull.at[c, k], gfull.at[c, k], g_sem, (k,), sibling)

    def adam(k):
        remote(gfull.at[1 - c, k], gfull.at[1 - c, k], g_sem, (k,), sibling).wait_recv()
        for h in range(2):
            cols = pl.ds(columns(k, h), w)
            v = gfull[h, k]
            g = jnp.where(c == 0, v[0:4], v[4:8])
            first = fbase[:, cols] + (1.0 - beta_one) * g
            second = sbase[:, cols] + (1.0 - beta_two) * g * g
            fbase[:, cols] = first
            sbase[:, cols] = second
            direction = first / corr_one / (jnp.sqrt(second / corr_two) + adam_eps)
            updated = master[:, cols] - rate * direction
            new_master[:, cols] = updated
            for q in range(2):
                r = 4 * (2 * h + q)
                slotf[r : r + 4, k * (w // 2) : (k + 1) * (w // 2)] = updated[
                    :, q * (w // 2) : (q + 1) * (w // 2)
                ]

    def quantize(k):
        for b in range(2 * nb):
            j = 2 * k * nb + b
            cols = pl.ds(j * BLOCK, BLOCK)
            first, second = fbase[:, cols], sbase[:, cols]
            peak = jnp.max(jnp.abs(first), axis=1, keepdims=True) + scale_eps
            new_fs[:, j : j + 1] = peak
            new_first[:, cols] = (first / peak).astype(bf16)
            peak = jnp.max(second, axis=1, keepdims=True) + scale_eps
            new_ss[:, j : j + 1] = peak
            new_second[:, cols] = (second / peak).astype(bf16)

    per = CHUNKS // GROUPS
    wide = per * (w // 2)
    half = wide // 2
    placed = []

    def place(e, yy, xx, cc, zz=None, lo=0, width=wide):
        row = pl.multiple_of(index(0, yy, xx, cc) * 4 * TILE, TILE)
        count = 4 * TILE
        if zz is not None:
            row, count = pl.multiple_of(row + zz * TILE, TILE), TILE
        return comm.at[pl.ds(row, count), pl.ds(e * wide + lo, width)]

    def gather_own(e):
        cols = pl.ds(e * wide, wide)
        slot[:, cols] = slotf[:, cols].astype(bf16)
        src, dst = slot.at[:, cols], place(e, y, x, c, z)
        for d in range(1, 4):
            send(src, dst, az_sem, (e, d), zn[d])
        placed.append(local(src, dst, loc_sem.at[e]))

    def gather_z(e):
        placed[e].wait()
        for d in range(1, 4):
            ref = place(e, y, x, c, z_from[d])
            remote(ref, ref, az_sem, (e, d), zn[d]).wait_recv()
        ref = place(e, y, x, c)
        send(ref, ref, ax_sem, (e,), xn)
        send(ref, ref, ay_sem, (e,), yn)
        send(ref, ref, as_sem, (e, 0), sibling)

    def gather_xy(e):
        ref = place(e, y, 1 - x, c)
        remote(ref, ref, ax_sem, (e,), xn).wait_recv()
        right = place(e, y, 1 - x, c, None, half, half)
        send(right, right, fy_sem, (e,), yn)
        other = place(e, 1 - y, x, c)
        remote(other, other, ay_sem, (e,), yn).wait_recv()
        left = place(e, 1 - y, x, c, None, 0, half)
        send(left, left, fx_sem, (e,), xn)
        send(ref, ref, as_sem, (e, 1), sibling)
        send(other, other, as_sem, (e, 2), sibling)

    def gather_far(e):
        left = place(e, 1 - y, 1 - x, c, None, 0, half)
        right = place(e, 1 - y, 1 - x, c, None, half, half)
        remote(left, left, fx_sem, (e,), xn).wait_recv()
        remote(right, right, fy_sem, (e,), yn).wait_recv()
        ref = place(e, 1 - y, 1 - x, c)
        send(ref, ref, as_sem, (e, 3), sibling)

    def gather_end(e):
        for q in range(4):
            yy = 1 - y if q >= 2 else y
            xx = 1 - x if q % 2 == 1 else x
            ref = place(e, yy, xx, 1 - c)
            remote(ref, ref, as_sem, (e, q), sibling).wait_recv()

    def chunks(e):
        return range(e * per, (e + 1) * per)

    def bases(e):
        for k in chunks(e):
            base(k)

    def step(e):
        for k in chunks(e):
            along_z(k)
        for k in chunks(e):
            adam(k)
        gather_own(e)
        for k in chunks(e):
            quantize(k)

    for e in range(2):
        for k in chunks(e):
            core_sum(k)
    for copy in fetched:
        copy.wait()
    bases(0)
    bases(1)
    for t in range(1, GROUPS + 6):
        if t - 1 < GROUPS:
            for k in chunks(t - 1):
                first_axis(k)
        if t + 1 < GROUPS:
            for k in chunks(t + 1):
                core_sum(k)
            bases(t + 1)
        if 0 <= t - 2 < GROUPS:
            for k in chunks(t - 2):
                second_axis(k)
        if 0 <= t - 3 < GROUPS:
            step(t - 3)
        if 0 <= t - 4 < GROUPS:
            gather_z(t - 4)
        if 0 <= t - 5 < GROUPS:
            gather_xy(t - 5)
        if 0 <= t - 6 < GROUPS:
            gather_far(t - 6)
    stored = [
        local(src, dst, out_sem.at[i])
        for i, (src, dst) in enumerate(
            (
                (new_master, master_out),
                (new_first, first_out),
                (new_fs, fs_out),
                (new_second, second_out),
                (new_ss, ss_out),
            )
        )
    ]
    for e in range(GROUPS):
        gather_end(e)
    for copy in sent:
        copy.wait_send()
    for copy in stored:
        copy.wait()


def exchange(grad, gscale, master, fm, fs, sm, ss):
    rows, d = grad.shape
    own_rows = master.shape[0]
    w = d // 2 // CHUNKS
    K, G = CHUNKS, GROUPS
    anywhere = pl.BlockSpec(memory_space=pl.ANY)
    dma = pltpu.SemaphoreType.DMA
    smalls = (master, fm, fs, sm, ss)
    return pl.pallas_call(
        exchange_kernel,
        out_shape=(jax.ShapeDtypeStruct((rows * 4, d // 4), bf16),)
        + tuple(jax.ShapeDtypeStruct(s.shape, s.dtype) for s in smalls),
        in_specs=[anywhere] * 7,
        out_specs=(anywhere,) * 6,
        scratch_shapes=[
            pltpu.VMEM((K, rows, w), bf16),
            pltpu.VMEM((K, rows, w), bf16),
            pltpu.VMEM(gscale.shape, bf16),
            pltpu.VMEM(gscale.shape, bf16),
            pltpu.VMEM((rows, gscale.shape[1] // 2), f32),
            pltpu.VMEM((rows, gscale.shape[1] // 2), f32),
            pltpu.VMEM((K, 2, 2, 4, 8, w), f32),
            pltpu.VMEM((K, 2, 4, 8, w), f32),
            pltpu.VMEM((K, 4, 8, w), f32),
            pltpu.VMEM((K, 4, 8, w), f32),
            pltpu.VMEM((K, 4, 8, w), f32),
            pltpu.VMEM((2, K, 8, w), f32),
            pltpu.VMEM((own_rows, d), f32),
            pltpu.VMEM((own_rows, d), f32),
            pltpu.VMEM((TILE, d // 4), f32),
            pltpu.VMEM((TILE, d // 4), bf16),
        ]
        + [pltpu.VMEM(s.shape, s.dtype) for s in smalls + smalls]
        + [
            dma((6,)),
            dma((5,)),
            dma((K,)),
            dma((2, 1)),
            dma((2, K)),
            dma((2, K)),
            dma((2, K)),
            dma((2, K, 4)),
            dma((2, K)),
            dma((2, G, 4)),
            dma((2, G)),
            dma((2, G)),
            dma((2, G)),
            dma((2, G)),
            dma((2, G, 4)),
            dma((G,)),
        ],
        compiler_params=pltpu.CompilerParams(
            collective_id=0, has_side_effects=True, vmem_limit_bytes=60 * 1024 * 1024
        ),
        cost_estimate=pl.CostEstimate(
            flops=8 * rows * d, bytes_accessed=8 * rows * d, transcendentals=own_rows * d
        ),
        name="exchange",
    )(grad, gscale, master, fm, fs, sm, ss)


def assemble_kernel(comm, *refs):
    smalls, (weights, transposed), copied = refs[:5], refs[5:7], refs[7:12]
    pick, eye, sem = refs[12:]
    t = pl.program_id(0)
    rows = weights.shape[0]
    cols = comm.shape[1]
    step = eye.shape[0]
    copies = [pltpu.make_async_copy(a, b, sem.at[i]) for i, (a, b) in enumerate(zip(smalls, copied))]

    @pl.when(t == 0)
    def _():
        for copy in copies:
            copy.start()
        row = lax.broadcasted_iota(jnp.int32, pick.shape, 0)
        col = lax.broadcasted_iota(jnp.int32, pick.shape, 1)
        kk, r = row // rows, lax.rem(row, rows)
        device = r // 4
        wanted = (lax.rem(device, 8) * 4 + device // 8) * TILE + 4 * kk + lax.rem(r, 4)
        pick[...] = jnp.where(col == wanted, 1.0, 0.0).astype(bf16)
        row = lax.broadcasted_iota(jnp.int32, eye.shape, 0)
        col = lax.broadcasted_iota(jnp.int32, eye.shape, 1)
        eye[...] = jnp.where(row == col, 1.0, 0.0).astype(bf16)

    sorted_rows = jnp.dot(pick[...], comm[...], preferred_element_type=f32).astype(bf16)
    for kk in range(4):
        weights[:, kk * cols : (kk + 1) * cols] = sorted_rows[kk * rows : (kk + 1) * rows]
    for i in range(4 * cols // step):
        turned = lax.dot_general(
            eye[...],
            weights[:, i * step : (i + 1) * step],
            (((1,), (1,)), ((), ())),
            preferred_element_type=f32,
        )
        transposed[i * step : (i + 1) * step, :] = turned.astype(bf16)

    @pl.when(t == pl.num_programs(0) - 1)
    def _():
        for copy in copies:
            copy.wait()


def assemble(comm, smalls):
    rows = comm.shape[0] // 4
    d = comm.shape[1] * 4
    cols = d // 4 // CHUNKS
    anywhere = pl.BlockSpec(memory_space=pl.ANY)
    return pl.pallas_call(
        assemble_kernel,
        grid=(CHUNKS,),
        out_shape=(
            jax.ShapeDtypeStruct((rows, d), bf16),
            jax.ShapeDtypeStruct((d, rows), bf16),
        )
        + tuple(jax.ShapeDtypeStruct(s.shape, s.dtype) for s in smalls),
        in_specs=[pl.BlockSpec((rows * 4, cols), lambda k: (0, k))] + [anywhere] * 5,
        out_specs=(
            pl.BlockSpec((rows, 4 * cols), lambda k: (0, k)),
            pl.BlockSpec((4 * cols, rows), lambda k: (k, 0)),
        )
        + (anywhere,) * 5,
        scratch_shapes=[
            pltpu.VMEM((rows * 4, rows * 4), bf16),
            pltpu.VMEM((256, 256), bf16),
            pltpu.SemaphoreType.DMA((5,)),
        ],
        compiler_params=pltpu.CompilerParams(
            vmem_limit_bytes=60 * 1024 * 1024,
            dimension_semantics=("arbitrary",),
        ),
        name="assemble",
    )(comm, *smalls)


def fused_on_device(
    grad_values, grad_scales, master, first_moment, first_scale, second_moment, second_scale
):
    def flat(array):
        return array.reshape(array.shape[-2:])

    comm, *smalls = exchange(
        flat(grad_values),
        flat(grad_scales),
        flat(master),
        flat(first_moment),
        flat(first_scale),
        flat(second_moment),
        flat(second_scale),
    )
    weights, transposed, *smalls = assemble(comm, smalls)
    return tuple(array[None] for array in (*smalls, weights, transposed))


def expand(values, scales):
    shape = values.shape
    blocks = values.astype(f32).reshape(shape[:-1] + (shape[-1] // BLOCK, BLOCK))
    return (blocks * scales.astype(f32)[..., None]).reshape(shape)


def quantize_blocks(values, signed):
    shape = values.shape
    blocks = values.reshape(shape[:-1] + (shape[-1] // BLOCK, BLOCK))
    if signed:
        peak = jnp.max(jnp.abs(blocks), axis=-1) + scale_eps
    else:
        peak = jnp.max(blocks, axis=-1) + scale_eps
    coded = (blocks / peak[..., None]).astype(bf16).reshape(shape)
    return (coded, peak)


def adam_step(gradient, master, first_moment, first_scale, second_moment, second_scale):
    first = beta_one * expand(first_moment, first_scale) + (1.0 - beta_one) * gradient
    second = beta_two * expand(second_moment, second_scale) + (1.0 - beta_two) * gradient * gradient
    direction = first / corr_one / (jnp.sqrt(second / corr_two) + adam_eps)
    updated = master - rate * direction
    first_coded, first_peak = quantize_blocks(first, True)
    second_coded, second_peak = quantize_blocks(second, False)
    return (updated, first_coded, first_peak, second_coded, second_peak, updated.astype(bf16))


def on_device(
    grad_values, grad_scales, master, first_moment, first_scale, second_moment, second_scale
):
    arrived, arrived_scales = (
        lax.all_to_all(grad_values, "group", split_axis=3, concat_axis=1, tiled=True),
        lax.all_to_all(grad_scales, "group", split_axis=3, concat_axis=1, tiled=True),
    )
    partial_sum = jnp.sum(expand(arrived, arrived_scales), axis=1)
    partial_sum = partial_sum.reshape(master.shape)
    gradient = lax.psum(partial_sum, "node")
    result = adam_step(gradient, master, first_moment, first_scale, second_moment, second_scale)
    updated, first_coded, first_peak, second_coded, second_peak, low_weights = result
    weights = lax.all_gather(low_weights, "group", axis=1, tiled=True)
    transposed = jnp.swapaxes(weights, 1, 2)
    return (updated, first_coded, first_peak, second_coded, second_peak, weights, transposed)


def solution(mesh):
    placed = (
        P("node", "group", "fsdp", None, None),
        P("node", "group", "fsdp", None, None),
        P("fsdp", "group", None),
        P("fsdp", "group", None),
        P("fsdp", "group", None),
        P("fsdp", "group", None),
        P("fsdp", "group", None),
    )
    fused = mesh.shape["node"] == 1 and mesh.shape["group"] == 32
    return jax.shard_map(
        fused_on_device if fused else on_device,
        mesh=mesh,
        in_specs=placed,
        out_specs=(
            P("fsdp", "group", None),
            P("fsdp", "group", None),
            P("fsdp", "group", None),
            P("fsdp", "group", None),
            P("fsdp", "group", None),
            P("fsdp", None, None),
            P("fsdp", None, None),
        ),
        check_vma=False,
    )
```

time: 89.6 us -> 81.4 us (0.908)
  local copies, waits for them, and re-layouts: 6.81 us -> 1.45 us
  Pallas kernels: 81.7 us -> 78.9 us
    pallas_call x1, Pallas kernels: 71 us -> 63.8 us  [exchange(): pl.pallas_call(exchange_kernel, out_shape=(jax.ShapeDtypeStruct((rows * 4...]
    unnamed x13 -> x1, local copies, waits for them, and re-layouts: 6.81 us -> 1.45 us
    pallas_call x1, Pallas kernels: 10.7 us -> 15.1 us  [assemble(): pl.pallas_call(assemble_kernel, grid=(CHUNKS,), out_shape=(jax.ShapeDtype...]
where the time goes in v2:
time: 81.4 us; the launch traced here: 81 us
  Pallas kernels  78.9 us (97%)
  local copies, waits for them, and re-layouts  1.45 us (2%)
    pallas_call x1, Pallas kernels, exchange(): pl.pallas_call(exchange_kernel, out_shape=(jax.ShapeDtypeStruct((rows * 4...  63.8 us
    pallas_call x1, Pallas kernels, assemble(): pl.pallas_call(assemble_kernel, grid=(CHUNKS,), out_shape=(jax.ShapeDtype...  15.1 us

profile of v2, /device:TPU:0, one launch (start us, length us, event | category | flops | bytes accessed | tf_op | source)
XLA Modules:
  0.0 81.0 jit_solution(2797808480829336946)
XLA Ops:
  0.6 1.5 %copy.14 = bf16[1,1,1,128,96]{4,3,2,1,0:T(8,128)(2,1)} copy(bf16[1,1,1,128,96]{3,4,2,1,0:T(8,128)(2,1)} %param.8) | data formatting | bytes 49152 | tf_op args[1]
  2.1 63.8 %exchange.1 = (bf16[512,3072]{1,0:T(8,128)(2,1)}, f32[4,12288]{1,0:T(4,128)}, bf16[4,12288]{1,0:T(4,128)(2,1)}, f32[4,96]{1,0:T(4,128)}, bf16[4,12288]{1,0:T(4,128)(2,1)}, /*index=5*/f32[4,96]{1,0:T(4,128)}) custom-call(bf16[128,12288]{1,0:T(8,128)(2,1)} %bitcast.14, bf16[128,96]{1,0:T(8,128)(2,1)} %bitcast.16, f32[4,12288]{1,0:T(4,128)} %bitcast.15, ...), custom_call_target="tpu_custom_call" | custom-call | flops 12582912 | bytes 12582912 | tf_op jit(solution)/shard_map/exchange/pallas_call | solution.py:333
  65.9 15.1 %assemble.1 = (bf16[128,12288]{1,0:T(8,128)(2,1)}, bf16[12288,128]{1,0:T(8,128)(2,1)}, f32[4,12288]{1,0:T(4,128)}, bf16[4,12288]{1,0:T(4,128)(2,1)}, f32[4,96]{1...) custom-call(bf16[512,3072]{1,0:T(8,128)(2,1)} %get-tuple-element.20.comm, f32[4,12288]{1,0:T(4,128)} %get-tuple-element.21.refs_0_, ...), custom_call_target="tpu_custom_call" | custom-call | tf_op jit(solution)/shard_map/assemble/pallas_call | solution.py:432

commit v3 on v2

--- a/solution.py
+++ b/solution.py
@@ -27,7 +27,7 @@
 def exchange_kernel(
     grad, gscale, master_in, fm_in, fs_in, sm_in, ss_in,
     comm, master_out, first_out, fs_out, second_out, ss_out,
-    own, sib, sc_own, sc_sib, sh_own, sh_sib, part, rx1, rx2, acc, rx3, gfull, fbase, sbase, slotf, slot,
+    own, sib, sc_own, sc_sib, sh_own, sh_sib, part, rx1, rx2, acc, rx3, gfull, fbase, sbase, slotf, slot, held,
     master, fm, fs, sm, ss, new_master, new_first, new_fs, new_second, new_ss,
     in_sem, out_sem, own_sem, sc_sem, sib_sem, p1_sem, p2_sem, z_sem, g_sem,
     az_sem, ax_sem, ay_sem, fx_sem, fy_sem, as_sem, loc_sem,
@@ -103,7 +103,7 @@
     ]
 
     def half_scales(ref, out):
-        values = ref[...].astype(f32)
+        values = ref[...].astype(f32).T
         for k in range(CHUNKS):
             j = 2 * k * nb
             out[:, k * nb : (k + 1) * nb] = jnp.where(
@@ -213,7 +213,7 @@
         count = 4 * TILE
         if zz is not None:
             row, count = pl.multiple_of(row + zz * TILE, TILE), TILE
-        return comm.at[pl.ds(row, count), pl.ds(e * wide + lo, width)]
+        return held.at[e, pl.ds(row, count), pl.ds(lo, width)]
 
     def gather_own(e):
         cols = pl.ds(e * wide, wide)
@@ -259,6 +259,7 @@
             xx = 1 - x if q % 2 == 1 else x
             ref = place(e, yy, xx, 1 - c)
             remote(ref, ref, as_sem, (e, q), sibling).wait_recv()
+        return local(held.at[e], comm.at[e], loc_sem.at[e])
 
     def chunks(e):
         return range(e * per, (e + 1) * per)
@@ -273,8 +274,6 @@
         for k in chunks(e):
             adam(k)
         gather_own(e)
-        for k in chunks(e):
-            quantize(k)
 
     for e in range(2):
         for k in chunks(e):
@@ -302,6 +301,9 @@
             gather_xy(t - 5)
         if 0 <= t - 6 < GROUPS:
             gather_far(t - 6)
+        if 0 <= t - 4 < GROUPS:
+            for k in chunks(t - 4):
+                quantize(k)
     stored = [
         local(src, dst, out_sem.at[i])
         for i, (src, dst) in enumerate(
@@ -315,7 +317,7 @@
         )
     ]
     for e in range(GROUPS):
-        gather_end(e)
+        stored.append(gather_end(e))
     for copy in sent:
         copy.wait_send()
     for copy in stored:
@@ -332,7 +334,7 @@
     smalls = (master, fm, fs, sm, ss)
     return pl.pallas_call(
         exchange_kernel,
-        out_shape=(jax.ShapeDtypeStruct((rows * 4, d // 4), bf16),)
+        out_shape=(jax.ShapeDtypeStruct((G, rows * 4, d // 4 // G), bf16),)
         + tuple(jax.ShapeDtypeStruct(s.shape, s.dtype) for s in smalls),
         in_specs=[anywhere] * 7,
         out_specs=(anywhere,) * 6,
@@ -341,8 +343,8 @@
             pltpu.VMEM((K, rows, w), bf16),
             pltpu.VMEM(gscale.shape, bf16),
             pltpu.VMEM(gscale.shape, bf16),
-            pltpu.VMEM((rows, gscale.shape[1] // 2), f32),
-            pltpu.VMEM((rows, gscale.shape[1] // 2), f32),
+            pltpu.VMEM((rows, gscale.shape[0] // 2), f32),
+            pltpu.VMEM((rows, gscale.shape[0] // 2), f32),
             pltpu.VMEM((K, 2, 2, 4, 8, w), f32),
             pltpu.VMEM((K, 2, 4, 8, w), f32),
             pltpu.VMEM((K, 4, 8, w), f32),
@@ -353,6 +355,7 @@
             pltpu.VMEM((own_rows, d), f32),
             pltpu.VMEM((TILE, d // 4), f32),
             pltpu.VMEM((TILE, d // 4), bf16),
+            pltpu.VMEM((G, rows * 4, d // 4 // G), bf16),
         ]
         + [pltpu.VMEM(s.shape, s.dtype) for s in smalls + smalls]
         + [
@@ -385,49 +388,57 @@
 
 def assemble_kernel(comm, *refs):
     smalls, (weights, transposed), copied = refs[:5], refs[5:7], refs[7:12]
-    pick, eye, sem = refs[12:]
+    eye, staged, in_sem, out_sem = refs[12], refs[13:18], refs[18], refs[19]
     t = pl.program_id(0)
-    rows = weights.shape[0]
-    cols = comm.shape[1]
+    cols = comm.shape[2]
     step = eye.shape[0]
-    copies = [pltpu.make_async_copy(a, b, sem.at[i]) for i, (a, b) in enumerate(zip(smalls, copied))]
+    loads = [pltpu.make_async_copy(a, b, in_sem.at[i]) for i, (a, b) in enumerate(zip(smalls, staged))]
+    stores = [pltpu.make_async_copy(a, b, out_sem.at[i]) for i, (a, b) in enumerate(zip(staged, copied))]
 
     @pl.when(t == 0)
     def _():
-        for copy in copies:
+        for copy in loads:
             copy.start()
-        row = lax.broadcasted_iota(jnp.int32, pick.shape, 0)
-        col = lax.broadcasted_iota(jnp.int32, pick.shape, 1)
-        kk, r = row // rows, lax.rem(row, rows)
-        device = r // 4
-        wanted = (lax.rem(device, 8) * 4 + device // 8) * TILE + 4 * kk + lax.rem(r, 4)
-        pick[...] = jnp.where(col == wanted, 1.0, 0.0).astype(bf16)
         row = lax.broadcasted_iota(jnp.int32, eye.shape, 0)
         col = lax.broadcasted_iota(jnp.int32, eye.shape, 1)
         eye[...] = jnp.where(row == col, 1.0, 0.0).astype(bf16)
 
-    sorted_rows = jnp.dot(pick[...], comm[...], preferred_element_type=f32).astype(bf16)
-    for kk in range(4):
-        weights[:, kk * cols : (kk + 1) * cols] = sorted_rows[kk * rows : (kk + 1) * rows]
+    @pl.when(t == 2)
+    def _():
+        for copy in loads:
+            copy.wait()
+        for copy in stores:
+            copy.start()
+
+    for z in range(4):
+        for u in range(2):
+            slots = [4 * (4 * u + i) + z for i in range(4)]
+            found = [comm[0, TILE * n : TILE * (n + 1), :].astype(f32) for n in slots]
+            row = 32 * z + 16 * u
+            for kk in range(4):
+                rows = jnp.concatenate([v[4 * kk : 4 * kk + 4] for v in found], axis=0)
+                weights[row : row + 16, kk * cols : (kk + 1) * cols] = rows.astype(bf16)
     for i in range(4 * cols // step):
-        turned = lax.dot_general(
-            eye[...],
-            weights[:, i * step : (i + 1) * step],
-            (((1,), (1,)), ((), ())),
-            preferred_element_type=f32,
-        )
+        block = weights[:, i * step : (i + 1) * step]
+        if i % 2 == 0:
+            turned = lax.dot_general(
+                eye[...], block, (((1,), (1,)), ((), ())), preferred_element_type=f32
+            )
+        else:
+            turned = block.astype(f32).T
         transposed[i * step : (i + 1) * step, :] = turned.astype(bf16)
 
     @pl.when(t == pl.num_programs(0) - 1)
     def _():
-        for copy in copies:
+        for copy in stores:
             copy.wait()
 
 
 def assemble(comm, smalls):
-    rows = comm.shape[0] // 4
-    d = comm.shape[1] * 4
+    rows = comm.shape[1] // 4
+    d = comm.shape[0] * comm.shape[2] * 4
     cols = d // 4 // CHUNKS
+    per = CHUNKS // GROUPS
     anywhere = pl.BlockSpec(memory_space=pl.ANY)
     return pl.pallas_call(
         assemble_kernel,
@@ -437,17 +448,16 @@
             jax.ShapeDtypeStruct((d, rows), bf16),
         )
         + tuple(jax.ShapeDtypeStruct(s.shape, s.dtype) for s in smalls),
-        in_specs=[pl.BlockSpec((rows * 4, cols), lambda k: (0, k))] + [anywhere] * 5,
+        in_specs=[pl.BlockSpec((1, rows * 4, cols), lambda k: (k // per, 0, lax.rem(k, per)))]
+        + [anywhere] * 5,
         out_specs=(
             pl.BlockSpec((rows, 4 * cols), lambda k: (0, k)),
             pl.BlockSpec((4 * cols, rows), lambda k: (k, 0)),
         )
         + (anywhere,) * 5,
-        scratch_shapes=[
-            pltpu.VMEM((rows * 4, rows * 4), bf16),
-            pltpu.VMEM((256, 256), bf16),
-            pltpu.SemaphoreType.DMA((5,)),
-        ],
+        scratch_shapes=[pltpu.VMEM((256, 256), bf16)]
+        + [pltpu.VMEM(s.shape, s.dtype) for s in smalls]
+        + [pltpu.SemaphoreType.DMA((5,)), pltpu.SemaphoreType.DMA((5,))],
         compiler_params=pltpu.CompilerParams(
             vmem_limit_bytes=60 * 1024 * 1024,
             dimension_semantics=("arbitrary",),
@@ -464,7 +474,7 @@
 
     comm, *smalls = exchange(
         flat(grad_values),
-        flat(grad_scales),
+        flat(grad_scales).T,
         flat(master),
         flat(first_moment),
         flat(first_scale),

time: 81.4 us -> 72.4 us (0.89)
  Pallas kernels: 78.9 us -> 71.5 us
  local copies, waits for them, and re-layouts: 1.45 us -> 0 us
    pallas_call x1, Pallas kernels: 15.1 us -> 7.86 us  [assemble(): pl.pallas_call(assemble_kernel, grid=(CHUNKS,), out_shape=(jax.ShapeDtype...]
    unnamed x1 -> x0, local copies, waits for them, and re-layouts: 1.45 us -> none
where the time goes in v3:
time: 72.4 us; the launch traced here: 72.1 us
  Pallas kernels  71.5 us (99%)
    pallas_call x1, Pallas kernels, exchange(): pl.pallas_call(exchange_kernel, out_shape=(jax.ShapeDtypeStruct((G, rows...  63.6 us
    pallas_call x1, Pallas kernels, assemble(): pl.pallas_call(assemble_kernel, grid=(CHUNKS,), out_shape=(jax.ShapeDtype...  7.86 us

profile of v3, /device:TPU:0, one launch (start us, length us, event | category | flops | bytes accessed | tf_op | source)
XLA Modules:
  0.0 72.1 jit_solution(10852591409220191059)
XLA Ops:
  0.6 63.6 %exchange.1 = (bf16[4,512,768]{2,1,0:T(8,128)(2,1)}, f32[4,12288]{1,0:T(4,128)}, bf16[4,12288]{1,0:T(4,128)(2,1)}, f32[4,96]{1,0:T(4,128)}, bf16[4,12288]{1,0:T(4,128)(2,1)}, /*index=5*/f32[4,96]{1,0:T(4,128)}) custom-call(bf16[128,12288]{1,0:T(8,128)(2,1)} %bitcast.16, bf16[96,128]{1,0:T(8,128)(2,1)} %bitcast.20, f32[4,12288]{1,0:T(4,128)} %bitcast.17, ...), custom_call_target="tpu_custom_call" | custom-call | flops 12582912 | bytes 12582912 | tf_op jit(solution)/shard_map/exchange/pallas_call | solution.py:335
  64.3 7.9 %assemble.1 = (bf16[128,12288]{1,0:T(8,128)(2,1)}, bf16[12288,128]{1,0:T(8,128)(2,1)}, f32[4,12288]{1,0:T(4,128)}, bf16[4,12288]{1,0:T(4,128)(2,1)}, f32[4,96]{1...) custom-call(bf16[4,512,768]{2,1,0:T(8,128)(2,1)} %get-tuple-element.20.comm, ...), custom_call_target="tpu_custom_call" | custom-call | tf_op jit(solution)/shard_map/assemble/pallas_call | solution.py:443

commit v4 on v3

--- a/solution.py
+++ b/solution.py
@@ -9,7 +9,7 @@
 
 BLOCK = 128
 CHUNKS = 8
-GROUPS = 4
+GROUPS = 8
 TILE = 16
 
 beta_one = 0.9
@@ -205,7 +205,7 @@
 
     per = CHUNKS // GROUPS
     wide = per * (w // 2)
-    half = wide // 2
+    nearly_half = [(wide // BLOCK + e % 2) // 2 * BLOCK for e in range(GROUPS)]
     placed = []
 
     def place(e, yy, xx, cc, zz=None, lo=0, width=wide):
@@ -236,18 +236,18 @@
     def gather_xy(e):
         ref = place(e, y, 1 - x, c)
         remote(ref, ref, ax_sem, (e,), xn).wait_recv()
-        right = place(e, y, 1 - x, c, None, half, half)
+        right = place(e, y, 1 - x, c, None, nearly_half[e], wide - nearly_half[e])
         send(right, right, fy_sem, (e,), yn)
         other = place(e, 1 - y, x, c)
         remote(other, other, ay_sem, (e,), yn).wait_recv()
-        left = place(e, 1 - y, x, c, None, 0, half)
+        left = place(e, 1 - y, x, c, None, 0, nearly_half[e])
         send(left, left, fx_sem, (e,), xn)
         send(ref, ref, as_sem, (e, 1), sibling)
         send(other, other, as_sem, (e, 2), sibling)
 
     def gather_far(e):
-        left = place(e, 1 - y, 1 - x, c, None, 0, half)
-        right = place(e, 1 - y, 1 - x, c, None, half, half)
+        left = place(e, 1 - y, 1 - x, c, None, 0, nearly_half[e])
+        right = place(e, 1 - y, 1 - x, c, None, nearly_half[e], wide - nearly_half[e])
         remote(left, left, fx_sem, (e,), xn).wait_recv()
         remote(right, right, fy_sem, (e,), yn).wait_recv()
         ref = place(e, 1 - y, 1 - x, c)
@@ -264,46 +264,34 @@
     def chunks(e):
         return range(e * per, (e + 1) * per)
 
-    def bases(e):
-        for k in chunks(e):
-            base(k)
-
-    def step(e):
-        for k in chunks(e):
-            along_z(k)
-        for k in chunks(e):
-            adam(k)
-        gather_own(e)
-
-    for e in range(2):
-        for k in chunks(e):
-            core_sum(k)
+    def each(f, e):
+        if 0 <= e < GROUPS:
+            for k in chunks(e):
+                f(k)
+
+    def group(f, e):
+        if 0 <= e < GROUPS:
+            f(e)
+
+    ahead = 4
+    for e in range(ahead):
+        each(core_sum, e)
     for copy in fetched:
         copy.wait()
-    bases(0)
-    bases(1)
-    for t in range(1, GROUPS + 6):
-        if t - 1 < GROUPS:
-            for k in chunks(t - 1):
-                first_axis(k)
-        if t + 1 < GROUPS:
-            for k in chunks(t + 1):
-                core_sum(k)
-            bases(t + 1)
-        if 0 <= t - 2 < GROUPS:
-            for k in chunks(t - 2):
-                second_axis(k)
-        if 0 <= t - 3 < GROUPS:
-            step(t - 3)
-        if 0 <= t - 4 < GROUPS:
-            gather_z(t - 4)
-        if 0 <= t - 5 < GROUPS:
-            gather_xy(t - 5)
-        if 0 <= t - 6 < GROUPS:
-            gather_far(t - 6)
-        if 0 <= t - 4 < GROUPS:
-            for k in chunks(t - 4):
-                quantize(k)
+    for e in range(ahead):
+        each(base, e)
+    for t in range(GROUPS + 7):
+        each(first_axis, t)
+        each(core_sum, t + ahead)
+        each(base, t + ahead)
+        each(second_axis, t - 2)
+        each(along_z, t - 3)
+        group(gather_far, t - 6)
+        group(gather_xy, t - 5)
+        each(adam, t - 3)
+        group(gather_own, t - 3)
+        group(gather_z, t - 4)
+        each(quantize, t - 5)
     stored = [
         local(src, dst, out_sem.at[i])
         for i, (src, dst) in enumerate(
@@ -425,7 +413,7 @@
                 eye[...], block, (((1,), (1,)), ((), ())), preferred_element_type=f32
             )
         else:
-            turned = block.astype(f32).T
+            turned = block.T
         transposed[i * step : (i + 1) * step, :] = turned.astype(bf16)
 
     @pl.when(t == pl.num_programs(0) - 1)

time: 72.4 us -> 77.2 us (1.066)
  Pallas kernels: 71.5 us -> 76.3 us
    pallas_call x1, Pallas kernels: 63.6 us -> 68.4 us  [exchange(): pl.pallas_call(exchange_kernel, out_shape=(jax.ShapeDtypeStruct((G, rows...]
where the time goes in v4:
time: 77.2 us; the launch traced here: 77 us
  Pallas kernels  76.3 us (99%)
    pallas_call x1, Pallas kernels, exchange(): pl.pallas_call(exchange_kernel, out_shape=(jax.ShapeDtypeStruct((G, rows...  68.4 us
    pallas_call x1, Pallas kernels, assemble(): pl.pallas_call(assemble_kernel, grid=(CHUNKS,), out_shape=(jax.ShapeDtype...  7.87 us

profile of v4, /device:TPU:0, one launch (start us, length us, event | category | flops | bytes accessed | tf_op | source)
XLA Modules:
  0.0 77.0 jit_solution(14389104537930232414)
XLA Ops:
  0.6 68.4 %exchange.1 = (bf16[8,512,384]{2,1,0:T(8,128)(2,1)}, f32[4,12288]{1,0:T(4,128)}, bf16[4,12288]{1,0:T(4,128)(2,1)}, f32[4,96]{1,0:T(4,128)}, bf16[4,12288]{1,0:T(4,128)(2,1)}, /*index=5*/f32[4,96]{1,0:T(4,128)}) custom-call(bf16[128,12288]{1,0:T(8,128)(2,1)} %bitcast.16, bf16[96,128]{1,0:T(8,128)(2,1)} %bitcast.20, f32[4,12288]{1,0:T(4,128)} %bitcast.17, ...), custom_call_target="tpu_custom_call" | custom-call | flops 12582912 | bytes 12582912 | tf_op jit(solution)/shard_map/exchange/pallas_call | solution.py:323
  69.1 7.9 %assemble.1 = (bf16[128,12288]{1,0:T(8,128)(2,1)}, bf16[12288,128]{1,0:T(8,128)(2,1)}, f32[4,12288]{1,0:T(4,128)}, bf16[4,12288]{1,0:T(4,128)(2,1)}, f32[4,96]{1...) custom-call(bf16[8,512,384]{2,1,0:T(8,128)(2,1)} %get-tuple-element.20.comm, ...), custom_call_target="tpu_custom_call" | custom-call | tf_op jit(solution)/shard_map/assemble/pallas_call | solution.py:431

commit v5 on v4

--- a/solution.py
+++ b/solution.py
@@ -9,7 +9,8 @@
 
 BLOCK = 128
 CHUNKS = 8
-GROUPS = 8
+PARTS = (0, 3, 5, 7, 8)
+GROUPS = len(PARTS) - 1
 TILE = 16
 
 beta_one = 0.9
@@ -203,22 +204,17 @@
             new_ss[:, j : j + 1] = peak
             new_second[:, cols] = (second / peak).astype(bf16)
 
-    per = CHUNKS // GROUPS
-    wide = per * (w // 2)
-    nearly_half = [(wide // BLOCK + e % 2) // 2 * BLOCK for e in range(GROUPS)]
+    wide = w // 2
     placed = []
 
-    def place(e, yy, xx, cc, zz=None, lo=0, width=wide):
-        row = pl.multiple_of(index(0, yy, xx, cc) * 4 * TILE, TILE)
-        count = 4 * TILE
-        if zz is not None:
-            row, count = pl.multiple_of(row + zz * TILE, TILE), TILE
-        return held.at[e, pl.ds(row, count), pl.ds(lo, width)]
+    def place(e, yy, xx, cc, first=0, count=4):
+        row = pl.multiple_of((index(0, yy, xx, cc) * 4 + first) * TILE, TILE)
+        return held.at[PARTS[e] : PARTS[e + 1], pl.ds(row, count * TILE)]
 
     def gather_own(e):
-        cols = pl.ds(e * wide, wide)
-        slot[:, cols] = slotf[:, cols].astype(bf16)
-        src, dst = slot.at[:, cols], place(e, y, x, c, z)
+        for k in chunks(e):
+            slot[k] = slotf[:, k * wide : (k + 1) * wide].astype(bf16)
+        src, dst = slot.at[PARTS[e] : PARTS[e + 1]], place(e, y, x, c, z, 1)
         for d in range(1, 4):
             send(src, dst, az_sem, (e, d), zn[d])
         placed.append(local(src, dst, loc_sem.at[e]))
@@ -226,7 +222,7 @@
     def gather_z(e):
         placed[e].wait()
         for d in range(1, 4):
-            ref = place(e, y, x, c, z_from[d])
+            ref = place(e, y, x, c, z_from[d], 1)
             remote(ref, ref, az_sem, (e, d), zn[d]).wait_recv()
         ref = place(e, y, x, c)
         send(ref, ref, ax_sem, (e,), xn)
@@ -236,18 +232,18 @@
     def gather_xy(e):
         ref = place(e, y, 1 - x, c)
         remote(ref, ref, ax_sem, (e,), xn).wait_recv()
-        right = place(e, y, 1 - x, c, None, nearly_half[e], wide - nearly_half[e])
+        right = place(e, y, 1 - x, c, 2, 2)
         send(right, right, fy_sem, (e,), yn)
         other = place(e, 1 - y, x, c)
         remote(other, other, ay_sem, (e,), yn).wait_recv()
-        left = place(e, 1 - y, x, c, None, 0, nearly_half[e])
+        left = place(e, 1 - y, x, c, 0, 2)
         send(left, left, fx_sem, (e,), xn)
         send(ref, ref, as_sem, (e, 1), sibling)
         send(other, other, as_sem, (e, 2), sibling)
 
     def gather_far(e):
-        left = place(e, 1 - y, 1 - x, c, None, 0, nearly_half[e])
-        right = place(e, 1 - y, 1 - x, c, None, nearly_half[e], wide - nearly_half[e])
+        left = place(e, 1 - y, 1 - x, c, 0, 2)
+        right = place(e, 1 - y, 1 - x, c, 2, 2)
         remote(left, left, fx_sem, (e,), xn).wait_recv()
         remote(right, right, fy_sem, (e,), yn).wait_recv()
         ref = place(e, 1 - y, 1 - x, c)
@@ -259,10 +255,11 @@
             xx = 1 - x if q % 2 == 1 else x
             ref = place(e, yy, xx, 1 - c)
             remote(ref, ref, as_sem, (e, q), sibling).wait_recv()
-        return local(held.at[e], comm.at[e], loc_sem.at[e])
+        part_of = slice(PARTS[e], PARTS[e + 1])
+        return local(held.at[part_of], comm.at[part_of], loc_sem.at[e])
 
     def chunks(e):
-        return range(e * per, (e + 1) * per)
+        return range(PARTS[e], PARTS[e + 1])
 
     def each(f, e):
         if 0 <= e < GROUPS:
@@ -273,25 +270,25 @@
         if 0 <= e < GROUPS:
             f(e)
 
-    ahead = 4
+    ahead = 2
     for e in range(ahead):
         each(core_sum, e)
     for copy in fetched:
         copy.wait()
     for e in range(ahead):
         each(base, e)
-    for t in range(GROUPS + 7):
+    for t in range(GROUPS + 5):
         each(first_axis, t)
         each(core_sum, t + ahead)
         each(base, t + ahead)
-        each(second_axis, t - 2)
-        each(along_z, t - 3)
-        group(gather_far, t - 6)
-        group(gather_xy, t - 5)
-        each(adam, t - 3)
-        group(gather_own, t - 3)
-        group(gather_z, t - 4)
-        each(quantize, t - 5)
+        each(second_axis, t - 1)
+        each(along_z, t - 2)
+        each(adam, t - 2)
+        group(gather_own, t - 2)
+        group(gather_z, t - 3)
+        group(gather_xy, t - 4)
+        group(gather_far, t - 5)
+        each(quantize, t - 3)
     stored = [
         local(src, dst, out_sem.at[i])
         for i, (src, dst) in enumerate(
@@ -322,7 +319,7 @@
     smalls = (master, fm, fs, sm, ss)
     return pl.pallas_call(
         exchange_kernel,
-        out_shape=(jax.ShapeDtypeStruct((G, rows * 4, d // 4 // G), bf16),)
+        out_shape=(jax.ShapeDtypeStruct((K, rows * 4, d // 4 // K), bf16),)
         + tuple(jax.ShapeDtypeStruct(s.shape, s.dtype) for s in smalls),
         in_specs=[anywhere] * 7,
         out_specs=(anywhere,) * 6,
@@ -342,8 +339,8 @@
             pltpu.VMEM((own_rows, d), f32),
             pltpu.VMEM((own_rows, d), f32),
             pltpu.VMEM((TILE, d // 4), f32),
-            pltpu.VMEM((TILE, d // 4), bf16),
-            pltpu.VMEM((G, rows * 4, d // 4 // G), bf16),
+            pltpu.VMEM((K, TILE, d // 4 // K), bf16),
+            pltpu.VMEM((K, rows * 4, d // 4 // K), bf16),
         ]
         + [pltpu.VMEM(s.shape, s.dtype) for s in smalls + smalls]
         + [
@@ -376,10 +373,10 @@
 
 def assemble_kernel(comm, *refs):
     smalls, (weights, transposed), copied = refs[:5], refs[5:7], refs[7:12]
-    eye, staged, in_sem, out_sem = refs[12], refs[13:18], refs[18], refs[19]
+    staged, in_sem, out_sem = refs[12:17], refs[17], refs[18]
     t = pl.program_id(0)
     cols = comm.shape[2]
-    step = eye.shape[0]
+    step = 2 * BLOCK
     loads = [pltpu.make_async_copy(a, b, in_sem.at[i]) for i, (a, b) in enumerate(zip(smalls, staged))]
     stores = [pltpu.make_async_copy(a, b, out_sem.at[i]) for i, (a, b) in enumerate(zip(staged, copied))]
 
@@ -387,9 +384,6 @@
     def _():
         for copy in loads:
             copy.start()
-        row = lax.broadcasted_iota(jnp.int32, eye.shape, 0)
-        col = lax.broadcasted_iota(jnp.int32, eye.shape, 1)
-        eye[...] = jnp.where(row == col, 1.0, 0.0).astype(bf16)
 
     @pl.when(t == 2)
     def _():
@@ -408,13 +402,7 @@
                 weights[row : row + 16, kk * cols : (kk + 1) * cols] = rows.astype(bf16)
     for i in range(4 * cols // step):
         block = weights[:, i * step : (i + 1) * step]
-        if i % 2 == 0:
-            turned = lax.dot_general(
-                eye[...], block, (((1,), (1,)), ((), ())), preferred_element_type=f32
-            )
-        else:
-            turned = block.T
-        transposed[i * step : (i + 1) * step, :] = turned.astype(bf16)
+        transposed[i * step : (i + 1) * step, :] = block.T
 
     @pl.when(t == pl.num_programs(0) - 1)
     def _():
@@ -426,7 +414,6 @@
     rows = comm.shape[1] // 4
     d = comm.shape[0] * comm.shape[2] * 4
     cols = d // 4 // CHUNKS
-    per = CHUNKS // GROUPS
     anywhere = pl.BlockSpec(memory_space=pl.ANY)
     return pl.pallas_call(
         assemble_kernel,
@@ -436,15 +423,14 @@
             jax.ShapeDtypeStruct((d, rows), bf16),
         )
         + tuple(jax.ShapeDtypeStruct(s.shape, s.dtype) for s in smalls),
-        in_specs=[pl.BlockSpec((1, rows * 4, cols), lambda k: (k // per, 0, lax.rem(k, per)))]
+        in_specs=[pl.BlockSpec((1, rows * 4, cols), lambda k: (k, 0, 0))]
         + [anywhere] * 5,
         out_specs=(
             pl.BlockSpec((rows, 4 * cols), lambda k: (0, k)),
             pl.BlockSpec((4 * cols, rows), lambda k: (k, 0)),
         )
         + (anywhere,) * 5,
-        scratch_shapes=[pltpu.VMEM((256, 256), bf16)]
-        + [pltpu.VMEM(s.shape, s.dtype) for s in smalls]
+        scratch_shapes=[pltpu.VMEM(s.shape, s.dtype) for s in smalls]
         + [pltpu.SemaphoreType.DMA((5,)), pltpu.SemaphoreType.DMA((5,))],
         compiler_params=pltpu.CompilerParams(
             vmem_limit_bytes=60 * 1024 * 1024,

time: 77.2 us -> 73 us (0.946)
  Pallas kernels: 76.3 us -> 72.1 us
    pallas_call x1, Pallas kernels: 68.4 us -> 64.6 us  [exchange(): pl.pallas_call(exchange_kernel, out_shape=(jax.ShapeDtypeStruct((K, rows...]
where the time goes in v5:
time: 73 us; the launch traced here: 72.7 us
  Pallas kernels  72.1 us (99%)
    pallas_call x1, Pallas kernels, exchange(): pl.pallas_call(exchange_kernel, out_shape=(jax.ShapeDtypeStruct((K, rows...  64.6 us
    pallas_call x1, Pallas kernels, assemble(): pl.pallas_call(assemble_kernel, grid=(CHUNKS,), out_shape=(jax.ShapeDtype...  7.45 us

profile of v5, /device:TPU:0, one launch (start us, length us, event | category | flops | bytes accessed | tf_op | source)
XLA Modules:
  0.0 72.7 jit_solution(12361225641641711458)
XLA Ops:
  0.6 64.6 %exchange.1 = (bf16[8,512,384]{2,1,0:T(8,128)(2,1)}, f32[4,12288]{1,0:T(4,128)}, bf16[4,12288]{1,0:T(4,128)(2,1)}, f32[4,96]{1,0:T(4,128)}, bf16[4,12288]{1,0:T(4,128)(2,1)}, /*index=5*/f32[4,96]{1,0:T(4,128)}) custom-call(bf16[128,12288]{1,0:T(8,128)(2,1)} %bitcast.16, bf16[96,128]{1,0:T(8,128)(2,1)} %bitcast.20, f32[4,12288]{1,0:T(4,128)} %bitcast.17, ...), custom_call_target="tpu_custom_call" | custom-call | flops 12582912 | bytes 12582912 | tf_op jit(solution)/shard_map/exchange/pallas_call | solution.py:320
  65.3 7.4 %assemble.1 = (bf16[128,12288]{1,0:T(8,128)(2,1)}, bf16[12288,128]{1,0:T(8,128)(2,1)}, f32[4,12288]{1,0:T(4,128)}, bf16[4,12288]{1,0:T(4,128)(2,1)}, f32[4,96]{1...) custom-call(bf16[8,512,384]{2,1,0:T(8,128)(2,1)} %get-tuple-element.20.comm, ...), custom_call_target="tpu_custom_call" | custom-call | tf_op jit(solution)/shard_map/assemble/pallas_call | solution.py:418

commit v6 on v5

--- a/solution.py
+++ b/solution.py
@@ -9,7 +9,7 @@
 
 BLOCK = 128
 CHUNKS = 8
-PARTS = (0, 3, 5, 7, 8)
+PARTS = (0, 3, 6, 8)
 GROUPS = len(PARTS) - 1
 TILE = 16
 

time: 73 us -> 74.3 us (1.018)
  Pallas kernels: 72.1 us -> 73.4 us
    pallas_call x1, Pallas kernels: 64.6 us -> 65.9 us  [exchange(): pl.pallas_call(exchange_kernel, out_shape=(jax.ShapeDtypeStruct((K, rows...]
where the time goes in v6:
time: 74.3 us; the launch traced here: 74 us
  Pallas kernels  73.4 us (99%)
    pallas_call x1, Pallas kernels, exchange(): pl.pallas_call(exchange_kernel, out_shape=(jax.ShapeDtypeStruct((K, rows...  65.9 us
    pallas_call x1, Pallas kernels, assemble(): pl.pallas_call(assemble_kernel, grid=(CHUNKS,), out_shape=(jax.ShapeDtype...  7.45 us

profile of v6, /device:TPU:0, one launch (start us, length us, event | category | flops | bytes accessed | tf_op | source)
XLA Modules:
  0.0 74.0 jit_solution(15244666039410979464)
XLA Ops:
  0.6 65.9 %exchange.1 = (bf16[8,512,384]{2,1,0:T(8,128)(2,1)}, f32[4,12288]{1,0:T(4,128)}, bf16[4,12288]{1,0:T(4,128)(2,1)}, f32[4,96]{1,0:T(4,128)}, bf16[4,12288]{1,0:T(4,128)(2,1)}, /*index=5*/f32[4,96]{1,0:T(4,128)}) custom-call(bf16[128,12288]{1,0:T(8,128)(2,1)} %bitcast.16, bf16[96,128]{1,0:T(8,128)(2,1)} %bitcast.20, f32[4,12288]{1,0:T(4,128)} %bitcast.17, ...), custom_call_target="tpu_custom_call" | custom-call | flops 12582912 | bytes 12582912 | tf_op jit(solution)/shard_map/exchange/pallas_call | solution.py:320
  66.6 7.4 %assemble.1 = (bf16[128,12288]{1,0:T(8,128)(2,1)}, bf16[12288,128]{1,0:T(8,128)(2,1)}, f32[4,12288]{1,0:T(4,128)}, bf16[4,12288]{1,0:T(4,128)(2,1)}, f32[4,96]{1...) custom-call(bf16[8,512,384]{2,1,0:T(8,128)(2,1)} %get-tuple-element.20.comm, ...), custom_call_target="tpu_custom_call" | custom-call | tf_op jit(solution)/shard_map/assemble/pallas_call | solution.py:418
